TPU v7x, 32 devices: a whole 2x2x4 slice. The times are simulated.
32 devices in a mesh: dp: 16 (over z, y, core), tile: 2 (over x).
Axes of the slice: x: 2, y: 2, z: 4, core: 2. Of those that a mesh axis runs over, the one named last changes fastest.
Arguments:
- frames: bfloat16 [16, 2, 3, 32, 128], P('dp', None, None, 'tile'), may hold values from 0 to 1
- features: bfloat16 [16, 64, 32, 128], P('dp', None, 'tile'), may hold values from -6 to 6
- cotangent: float32 [16, 3, 32, 128], P('dp', None, 'tile'), may hold values from -6 to 6
- head_weight: bfloat16 [108, 576], replicated, may hold values from -0.25 to 0.25
Outputs:
- grad_weight: float32 [108, 576], replicated
- grad_features: float32 [16, 64, 32, 128], P('dp', None, 'tile')
- grad_frames: float32 [16, 2, 3, 32, 128], P('dp', None, None, 'tile')
All inputs are finite; a program needn't handle non-finite values.
Results may differ from a plain program's by a relative error of at most 0.003.
Values may be sent and summed in bfloat16 or wider, within the bound.
A program may use at most 64 MiB of HBM per device.

v0:
```python
import jax
import jax.numpy as jnp
from jax import lax
from jax.sharding import PartitionSpec as P


def with_halo(cells, sides, width):
    for axis, dim in sides:
        count = lax.axis_size(axis)
        ends = count - 1
        head = lax.slice_in_dim(cells, 0, width, axis=dim)
        tail = lax.slice_in_dim(cells, cells.shape[dim] - width, cells.shape[dim], axis=dim)
        cells = jnp.concatenate(
            [
                lax.ppermute(tail, axis, [(i, (i + 1) % count) for i in range(ends)]),
                cells,
                lax.ppermute(head, axis, [((i + 1) % count, i) for i in range(ends)]),
            ],
            axis=dim,
        )
    return cells


def from_behind(value, axis, steps):
    count = lax.axis_size(axis)
    leading, last = (max(0, -steps), min(count, count - steps))
    return lax.ppermute(value, axis, [(source, source + steps) for source in range(leading, last)])


def make_patches(padded_map, row_count, col_count):
    blocks = []
    for row_shift in range(3):
        for col_shift in range(3):
            piece = padded_map[
                :, row_shift : row_shift + row_count, col_shift : col_shift + col_count
            ]
            blocks.append(piece.reshape(piece.shape[0], row_count * col_count))
    return jnp.concatenate(blocks, 0)


def fold_patches(patch_grad, channels, row_count, col_count):
    folded = jnp.zeros((channels, row_count + 2, col_count + 2), jnp.float32)
    slot_index = 0
    for row_shift in range(3):
        for col_shift in range(3):
            block = patch_grad[slot_index * channels : (slot_index + 1) * channels].reshape(
                channels, row_count, col_count
            )
            folded = folded.at[
                :, row_shift : row_shift + row_count, col_shift : col_shift + col_count
            ].add(block)
            slot_index += 1
    return folded


def separable_grads(padded, vertical, horizontal, upstream, group_size):
    tap_count = vertical.shape[0]
    row_count = upstream.shape[1]
    col_count = upstream.shape[2]

    def one_tap(tap_index, carried):
        grad_vert, grad_horiz, grad_padded = carried
        tap_band = lax.dynamic_slice_in_dim(padded, tap_index, row_count, 1)
        scaled = lax.dynamic_index_in_dim(vertical, tap_index, 0, keepdims=False)[None] * upstream
        blended = jnp.zeros(upstream.shape, jnp.float32)
        back_sum = jnp.zeros((3, row_count, col_count + tap_count - 1), jnp.float32)
        horiz_rows = []
        for col_tap in range(tap_count):
            shifted = tap_band[:, :, col_tap : col_tap + col_count]
            weight_row = horizontal[col_tap][None]
            blended = blended + weight_row * shifted
            horiz_rows.append(jnp.sum(scaled * shifted, 0))
            back_sum = back_sum + jnp.pad(
                weight_row * scaled, ((0, 0), (0, 0), (col_tap, tap_count - 1 - col_tap))
            )
        grad_vert = lax.dynamic_update_slice_in_dim(
            grad_vert, jnp.sum(upstream * blended, 0)[None], tap_index, 0
        )
        grad_horiz = grad_horiz + jnp.stack(horiz_rows)
        old_rows = lax.dynamic_slice_in_dim(grad_padded, tap_index, row_count, 1)
        grad_padded = lax.dynamic_update_slice_in_dim(
            grad_padded, old_rows + back_sum, tap_index, 1
        )
        return (grad_vert, grad_horiz, grad_padded)

    def group_step(group_index, carried):
        for offset in range(group_size):
            carried = one_tap(group_index * group_size + offset, carried)
        return carried

    start_state = (
        jnp.zeros(vertical.shape, jnp.float32),
        jnp.zeros(vertical.shape, jnp.float32),
        jnp.zeros(padded.shape, jnp.float32),
    )
    return lax.fori_loop(0, tap_count // group_size, group_step, start_state)


def shards(frames, features, cotangent, head_weight):
    tap_count = head_weight.shape[0] // 4
    rim_rows = (tap_count - 1) // 2
    kernel_scale = tap_count ** (-0.5)
    feature_map = features[0]
    channels, row_count, col_count = feature_map.shape
    upstream = cotangent[0]
    feature_ext = with_halo(feature_map, (("tile", 1),), 1)
    frame_ext = with_halo(frames[0], (("tile", 2),), rim_rows)
    patches = make_patches(jnp.pad(feature_ext, ((0, 0), (0, 0), (1, 1))), row_count, col_count)
    kernels = jnp.dot(head_weight, patches, preferred_element_type=jnp.float32).reshape(
        -1, row_count, col_count
    )
    grad_list = []
    frame_list = []
    for which_frame in range(2):
        vertical = (
            kernels[2 * which_frame * tap_count : (2 * which_frame + 1) * tap_count] * kernel_scale
        )
        horizontal = (
            kernels[(2 * which_frame + 1) * tap_count : (2 * which_frame + 2) * tap_count]
            * kernel_scale
        )
        padded = jnp.pad(
            frame_ext[which_frame].astype(jnp.float32), ((0, 0), (0, 0), (rim_rows, rim_rows))
        )
        grad_vert, grad_horiz, grad_padded = separable_grads(
            padded, vertical, horizontal, upstream, 3
        )
        grad_list += [grad_vert, grad_horiz]
        frame_list.append(grad_padded[:, :, rim_rows : rim_rows + col_count])
    kernel_grad = (jnp.concatenate(grad_list, 0) * kernel_scale).astype(jnp.bfloat16)
    out_channels = kernel_grad.shape[0]
    flat_grad = kernel_grad.reshape(out_channels, row_count * col_count)
    weight_part = lax.dot_general(
        flat_grad, patches, (((1,), (1,)), ((), ())), preferred_element_type=jnp.float32
    )
    weight_share = lax.psum_scatter(weight_part, "tile", scatter_dimension=1, tiled=True)
    weight_share = lax.psum(weight_share, "dp")
    weight_sum = lax.all_gather(weight_share, "tile", axis=1, tiled=True)
    pixel_count = lax.axis_size("dp") * lax.axis_size("tile") * row_count * col_count
    weight_sum = weight_sum * pixel_count ** (-0.5)
    image_grad = jnp.stack(frame_list)
    top_rim = image_grad[:, :, :rim_rows]
    bottom_rim = image_grad[:, :, rim_rows + row_count :]
    middle = image_grad[:, :, rim_rows : rim_rows + row_count]
    patch_grad = lax.dot_general(
        head_weight, flat_grad, (((0,), (0,)), ((), ())), preferred_element_type=jnp.float32
    )
    feature_pad = fold_patches(patch_grad, channels, row_count, col_count)[:, :, 1 : col_count + 1]
    from_above = from_behind((bottom_rim, feature_pad[:, row_count + 1 :]), "tile", 1)
    from_below = from_behind((top_rim, feature_pad[:, :1]), "tile", -1)
    feat_grad = feature_pad[:, 1 : row_count + 1]
    feat_grad = feat_grad.at[:, :1].add(from_above[1]).at[:, row_count - 1 :].add(from_below[1])
    above_image = from_above[0]
    below_image = from_below[0]
    middle = (
        middle.at[:, :, :rim_rows]
        .add(above_image)
        .at[:, :, row_count - rim_rows :]
        .add(below_image)
    )
    return (weight_sum, feat_grad[None], middle[None])


def solution(mesh):
    in_specs = (
        P("dp", None, None, "tile", None),
        P("dp", None, "tile", None),
        P("dp", None, "tile", None),
        P(),
    )
    out_specs = (P(), P("dp", None, "tile", None), P("dp", None, None, "tile", None))
    return jax.shard_map(shards, mesh=mesh, in_specs=in_specs, out_specs=out_specs, check_vma=False)
```

profile of v0, /device:TPU:0, one launch (start us, length us, event | category | flops | bytes accessed | tf_op | source)
XLA Modules:
  0.0 391.6 jit_solution(14271029286486155295)
XLA Ops:
  8.1 4.8 %collective-permute-start.2 = (bf16[2,3,13,128]{3,2,1,0:T(8,128)(2,1)S(1)}, bf16[2,3,13,128]{3,2,1,0:T(8,128)(2,1)S(1)}, u32[]{:S(2)}, u32[]{:S(2)}) collective-permute-start(bf16[2,3,13,128]{3,2,1,0:T(8,128)(2,1)S(1)} %get-tuple-element.1181), channel_id=1, source_target_pairs={{0,1},{2,3},{4,5},{6,7},{8,9},{10,11},{12,13},{14,15},{16,17},{18,... | collective-permute-start | bytes 59912 | tf_op jit(solution)/shard_map/ppermute | solution.py:15
  12.9 1.3 collective-permute-start.3
  14.2 1.0 fusion.30
  15.2 4.5 %collective-permute-start = (bf16[64,1,128]{2,1,0:T(2,128)(2,1)S(1)}, bf16[64,1,128]{2,1,0:T(2,128)(2,1)S(1)}, u32[]{:S(2)}, u32[]{:S(2)}) collective-permute-start(bf16[64,1,128]{2,1,0:T(2,128)(2,1)S(1)} %get-tuple-element.1175), channel_id=1, source_target_pairs={{0,1},{2,3},{4,5},{6,7},{8,9},{10,11},{12,13},{14,15},{16,17},{18,... | collective-permute-start | bytes 49160 | tf_op jit(solution)/shard_map/ppermute | solution.py:15
  19.8 1.3 collective-permute-start.1
  21.8 1.4 and_reduce_fusion
  23.8 1.8 collective-permute-done.1
  25.6 1.6 fusion.16
  31.4 59.1 %while.54 = (s32[]{:T(128)}, f32[27,16,128]{2,1,0:T(8,128)S(1)}, f32[27,16,128]{2,1,0:T(8,128)S(1)}, f32[3,42,154]{2,1,0:T(8,128)S(1)}, f32[27,16,128]{2,1,0:T(8...) while((s32[]{:T(128)}, f32[27,16,128]{2,1,0:T(8,128)S(1)}, ...), condition=%wide.region_171.172_spmd.clone, body=%wide.region_86.171_spmd.clone.sunk | while | flops 3173135 | bytes 13660168 | solution.py:96
  92.9 129.1 %while.53 = (s32[]{:T(128)}, f32[27,16,128]{2,1,0:T(8,128)}, f32[27,16,128]{2,1,0:T(8,128)S(1)}, f32[3,42,154]{2,1,0:T(8,128)S(1)}, f32[27,16,128]{2,1,0:T(8,128...) while((s32[]{:T(128)}, f32[27,16,128]{2,1,0:T(8,128)}, ...), condition=%wide.region_85.86_spmd.clone, body=%wide.region_0.85_spmd.clone.sunk | while | flops 3173135 | bytes 13856832 | solution.py:96
  92.9 0.9 fusion.42
  98.6 1.0 multiply_reduce_fusion.186
  102.1 0.8 broadcast_multiply_fusion.188
  103.7 1.5 add_add_fusion.13
  105.6 1.4 add_add_fusion.14
  112.9 1.0 multiply_reduce_fusion.186
  118.1 1.5 add_add_fusion.13
  119.9 1.4 add_add_fusion.14
  127.2 1.0 multiply_reduce_fusion.186
  132.4 1.5 add_add_fusion.13
  134.2 1.4 add_add_fusion.14
  141.5 1.0 multiply_reduce_fusion.186
  145.0 0.8 broadcast_multiply_fusion.188
  146.7 1.5 add_add_fusion.13
  148.5 1.4 add_add_fusion.14
  155.8 1.0 multiply_reduce_fusion.186
  161.0 1.5 add_add_fusion.13
  162.8 1.4 add_add_fusion.14
  170.1 1.0 multiply_reduce_fusion.186
  175.3 1.5 add_add_fusion.13
  177.1 1.4 add_add_fusion.14
  184.4 1.0 multiply_reduce_fusion.186
  189.6 1.5 add_add_fusion.13
  191.5 1.4 add_add_fusion.14
  198.8 1.0 multiply_reduce_fusion.186
  203.9 1.5 add_add_fusion.13
  205.8 1.4 add_add_fusion.14
  213.1 1.0 multiply_reduce_fusion.186
  218.2 1.5 add_add_fusion.13
  220.0 1.4 add_add_fusion.14
  222.0 1.0 pad.1903
  223.9 2.6 fusion.26
  226.5 1.9 convolution_bitcast_fusion
  229.2 1.6 slice_bitcast_fusion.54
  231.0 2.3 bitcast_add_fusion.6
  233.2 6.0 %scatter-add.45 = f32[64,18,130]{2,0,1:T(8,128)S(1)} dynamic-update-slice(f32[64,18,130]{2,0,1:T(8,128)S(1)} %scatter-add.44, f32[64,16,128]{2,0,1:T(8,128)} %bitcast_add_fusion.6, s32[]{:T(128)} %constant.559.clone.1, s32[]{:T(128)} %bitcast.7, s32[]{:T(128)} %bitcast.8) | dynamic-update-slice | bytes 1048580 | tf_op jit(solution)/shard_map/scatter-add | solution.py:51
  239.2 3.2 add_select_fusion
  242.4 5.2 %scatter-add.46 = f32[64,18,130]{2,0,1:T(8,128)S(1)} dynamic-update-slice(f32[64,18,130]{2,0,1:T(8,128)S(1)} %scatter-add.45, f32[64,16,128]{2,0,1:T(8,128)S(1)} %add_select_fusion, s32[]{:T(128)} %constant.559.clone.1, s32[]{:T(128)} %bitcast.9, s32[]{:T(128)} %bitcast.10) | dynamic-update-slice | bytes 1048580 | tf_op jit(solution)/shard_map/scatter-add | solution.py:51
  247.6 1.2 fusion.18
  248.8 2.1 bitcast_add_fusion.4
  250.9 4.7 %scatter-add.50 = f32[64,18,130]{2,0,1:T(8,128)S(1)} dynamic-update-slice(f32[64,18,130]{2,0,1:T(8,128)S(1)} %fusion.18, f32[64,16,128]{2,0,1:T(8,128)} %bitcast_add_fusion.4, s32[]{:T(128)} %constant.559.clone.1, s32[]{:T(128)} %constant.568.clone.1, s32[]{:T(128)} %constant.568.clone.1) | dynamic-update-slice | bytes 1048580 | tf_op jit(solution)/shard_map/scatter-add | solution.py:51
  255.6 1.0 bitcast_add_fusion.3
  256.6 4.7 %scatter-add.51 = f32[64,18,130]{2,0,1:T(8,128)S(1)} dynamic-update-slice(f32[64,18,130]{2,0,1:T(8,128)S(1)} %scatter-add.50, f32[64,16,128]{2,0,1:T(8,128)} %bitcast_add_fusion.3, s32[]{:T(128)} %constant.559.clone.1, s32[]{:T(128)} %constant.568.clone.1, s32[]{:T(128)} %constant.565.clone.1) | dynamic-update-slice | bytes 1048580 | tf_op jit(solution)/shard_map/scatter-add | solution.py:51
  261.6 3.9 scatter-add.55
  265.7 3.9 scatter-add.56
  269.6 2.8 collective-permute-start.4
  272.7 1.3 collective-permute-start.6
  274.0 1.3 collective-permute-start.5
  275.7 1.3 collective-permute-start.7
  277.0 2.8 collective-permute-done.5
  280.5 6.0 %reduce-scatter.2.cloned.1.call-done = f32[108,288]{0,1:T(8,128)} async-done(((f32[108,576]{0,1:T(8,128)}), f32[108,288]{0,1:T(8,128)}) %reduce-scatter.2.cloned.1.call-update) | async-done | bytes 124432 | tf_op jit(solution)/shard_map/reduce_scatter | solution.py:136
  286.7 90.9 %all-reduce.168.cloned.1.call-done = f32[108,288]{0,1:T(8,128)} async-done(((f32[108,288]{0,1:T(8,128)}), f32[108,288]{0,1:T(8,128)}) %all-reduce.168.cloned.1.call-update) | async-done | bytes 124432 | tf_op jit(solution)/shard_map/psum | solution.py:137
  377.7 6.2 %all_gather.3 = f32[108,576]{0,1:T(8,128)S(1)} all-gather(f32[108,288]{0,1:T(8,128)} %all-reduce.168.cloned.1.call-done), channel_id=1, replica_groups=mesh['dp'=16,'tile'=2] {'tile'}, dimensions={1}, use_global_device_ids=true | all-gather | bytes 373248 | tf_op jit(solution)/shard_map/all_gather | solution.py:138
  383.9 0.9 copy.17
  (2000 shorter events, 148.6 us)
Async XLA Ops:
  7.2 21.4 %copy-start = (bf16[108,576]{1,0:T(8,128)(2,1)S(1)}, bf16[108,576]{1,0:T(8,128)(2,1)}, u32[]{:S(2)}) copy-start(bf16[108,576]{1,0:T(8,128)(2,1)} %param.37) | copy-start | bytes 373252
  7.2 279.3 %reduce-scatter.2.cloned.1.call-start = ((), (), s32[]{:S(2)}) async-start(), calls=%async_computation.1 | async-start | bytes 442368 | tf_op jit(solution)/shard_map/reduce_scatter | solution.py:136
  8.1 23.1 %collective-permute-start.2 = (bf16[2,3,13,128]{3,2,1,0:T(8,128)(2,1)S(1)}, bf16[2,3,13,128]{3,2,1,0:T(8,128)(2,1)S(1)}, u32[]{:S(2)}, u32[]{:S(2)}) collective-permute-start(bf16[2,3,13,128]{3,2,1,0:T(8,128)(2,1)S(1)} %get-tuple-element.1181), channel_id=1, source_target_pairs={{0,1},{2,3},{4,5},{6,7},{8,9},{10,11},{12,13},{14,15},{16,17},{18,... | collective-permute-start | bytes 59912 | tf_op jit(solution)/shard_map/ppermute | solution.py:15
  12.9 18.3 %collective-permute-start.3 = (bf16[2,3,13,128]{3,2,1,0:T(8,128)(2,1)S(1)}, bf16[2,3,13,128]{3,2,1,0:T(8,128)(2,1)S(1)}, u32[]{:S(2)}, u32[]{:S(2)}) collective-permute-start(bf16[2,3,13,128]{3,2,1,0:T(8,128)(2,1)S(1)} %get-tuple-element.1182), channel_id=1, source_target_pairs={{1,0},{3,2},{5,4},{7,6},{9,8},{11,10},{13,12},{15,14},{17,16},{19,... | collective-permute-start | bytes 59912 | tf_op jit(solution)/shard_map/ppermute | solution.py:17
  15.2 8.5 %collective-permute-start = (bf16[64,1,128]{2,1,0:T(2,128)(2,1)S(1)}, bf16[64,1,128]{2,1,0:T(2,128)(2,1)S(1)}, u32[]{:S(2)}, u32[]{:S(2)}) collective-permute-start(bf16[64,1,128]{2,1,0:T(2,128)(2,1)S(1)} %get-tuple-element.1175), channel_id=1, source_target_pairs={{0,1},{2,3},{4,5},{6,7},{8,9},{10,11},{12,13},{14,15},{16,17},{18,... | collective-permute-start | bytes 49160 | tf_op jit(solution)/shard_map/ppermute | solution.py:15
  19.8 5.8 %collective-permute-start.1 = (bf16[64,1,128]{2,1,0:T(2,128)(2,1)S(1)}, bf16[64,1,128]{2,1,0:T(2,128)(2,1)S(1)}, u32[]{:S(2)}, u32[]{:S(2)}) collective-permute-start(bf16[64,1,128]{2,1,0:T(2,128)(2,1)S(1)} %get-tuple-element.1176), channel_id=1, source_target_pairs={{1,0},{3,2},{5,4},{7,6},{9,8},{11,10},{13,12},{15,14},{17,16},{19,... | collective-permute-start | bytes 49160 | tf_op jit(solution)/shard_map/ppermute | solution.py:17
  23.8 4.1 %copy-start.6 = (bf16[1,64,16,128]{3,2,1,0:T(8,128)(2,1)S(1)}, bf16[1,64,16,128]{3,2,1,0:T(8,128)(2,1)}, u32[]{:S(2)}) copy-start(bf16[1,64,16,128]{3,2,1,0:T(8,128)(2,1)} %param.35) | copy-start | bytes 786436
  28.6 1.4 copy-start.2
  30.1 1.0 copy-start.16
  30.1 1.2 copy-start.1
  90.5 2.3 copy-start.4
  92.9 131.0 %copy-start.3 = (bf16[576,2048]{1,0:T(8,128)(2,1)S(1)}, bf16[576,2048]{1,0:T(8,128)(2,1)}, u32[]{:S(2)}) copy-start(bf16[576,2048]{1,0:T(8,128)(2,1)} %copy-done.2) | copy-start | bytes 7077892
  102.1 3.5 copy-start.7
  102.9 2.6 copy-start.8
  116.4 3.5 copy-start.7
  117.2 2.6 copy-start.8
  130.7 3.5 copy-start.7
  131.6 2.6 copy-start.8
  145.0 3.5 copy-start.7
  145.9 2.6 copy-start.8
  159.3 3.5 copy-start.7
  160.2 2.6 copy-start.8
  173.7 3.5 copy-start.7
  174.5 2.6 copy-start.8
  188.0 3.5 copy-start.7
  188.8 2.6 copy-start.8
  202.3 3.5 copy-start.7
  203.1 2.6 copy-start.8
  216.6 3.4 copy-start.7
  217.4 2.6 copy-start.8
  223.0 0.7 copy-start.13
  223.1 3.4 copy-start.11
  223.1 3.4 copy-start.12
  223.2 0.7 copy-start.14
  226.5 1.9 copy-start.5
  247.6 8.0 %copy-start.9 = (f32[8,16,8,128]{3,2,1,0:T(8,128)S(1)}, f32[8,16,8,128]{3,2,1,0:T(8,128)}, u32[]{:S(2)}) copy-start(f32[8,16,8,128]{3,2,1,0:T(8,128)} %get-tuple-element.1155) | copy-start | bytes 1572868
  261.4 11.0 %copy-start.10 = (f32[1,3,42,128]{3,2,1,0:T(8,128)S(1)}, f32[1,3,42,128]{3,2,1,0:T(8,128)}, u32[]{:S(2)}) copy-start(f32[1,3,42,128]{3,2,1,0:T(8,128)} %slice_bitcast_fusion.64) | copy-start | bytes 193540
  269.6 5.7 %collective-permute-start.4 = (f32[64,1,128]{2,0,1:T(8,128)S(1)}, f32[64,1,128]{2,0,1:T(8,128)S(1)}, u32[]{:S(2)}, u32[]{:S(2)}) collective-permute-start(f32[64,1,128]{2,0,1:T(8,128)S(1)} %get-tuple-element.1162), channel_id=1, source_target_pairs={{0,1},{2,3},{4,5},{6,7},{8,9},{10,11},{12,13},{14,15},{16,17},{18,... | collective-permute-start | bytes 98312 | tf_op jit(solution)/shard_map/ppermute | solution.py:27
  272.7 3.0 collective-permute-start.6
  274.0 103.7 %all-reduce.168.cloned.1.call-start = ((), (), s32[]{:S(2)}) async-start(), calls=%async_computation.2 | async-start | bytes 294912 | tf_op jit(solution)/shard_map/psum | solution.py:137
  274.0 5.8 %collective-permute-start.5 = (f32[64,1,128]{2,0,1:T(8,128)S(1)}, f32[64,1,128]{2,0,1:T(8,128)S(1)}, u32[]{:S(2)}, u32[]{:S(2)}) collective-permute-start(f32[64,1,128]{2,0,1:T(8,128)S(1)} %get-tuple-element.1161), channel_id=1, source_target_pairs={{1,0},{3,2},{5,4},{7,6},{9,8},{11,10},{13,12},{15,14},{17,16},{19,... | collective-permute-start | bytes 98312 | tf_op jit(solution)/shard_map/ppermute | solution.py:27
  275.7 10.8 %collective-permute-start.7 = (f32[2,3,13,128]{3,2,1,0:T(8,128)S(1)}, f32[2,3,13,128]{3,2,1,0:T(8,128)S(1)}, u32[]{:S(2)}, u32[]{:S(2)}) collective-permute-start(f32[2,3,13,128]{3,2,1,0:T(8,128)S(1)} %get-tuple-element.1177), channel_id=1, source_target_pairs={{1,0},{3,2},{5,4},{7,6},{9,8},{11,10},{13,12},{15,14},{17,16},{19,... | collective-permute-start | bytes 119816 | tf_op jit(solution)/shard_map/ppermute | solution.py:27
  280.3 104.4 %copy-start.15 = (f32[1,64,16,128]{3,2,1,0:T(8,128)}, f32[1,64,16,128]{3,2,1,0:T(8,128)S(1)}, u32[]{:S(2)}) copy-start(f32[1,64,16,128]{3,2,1,0:T(8,128)S(1)} %scatter-add.60) | copy-start | bytes 1572868
  286.7 98.0 %copy-start.17 = (f32[1,2,3,16,128]{4,3,2,1,0:T(8,128)}, f32[1,2,3,16,128]{4,3,2,1,0:T(8,128)S(1)}, u32[]{:S(2)}) copy-start(f32[1,2,3,16,128]{4,3,2,1,0:T(8,128)S(1)} %scatter-add.64) | copy-start | bytes 147460
Sparse Core Ops, SparseCore 0:
  274.1 12.3 reduce-scatter.1
  289.9 87.6 all-reduce.167
where the time goes:
time: 394 us; the launch traced here: 392 us
  other arithmetic  143 us (36%)
  waiting for transfers between devices  102 us (26%)
  local copies, waits for them, and re-layouts  87.6 us (22%)
  starting transfers between devices  18.7 us (5%)
  between operations  14.7 us (4%)
  loops' own time  14.3 us (4%)
  blocking collectives  6.18 us (2%)
  matrix products  5.03 us (1%)
    psum x1, waiting for transfers between devices, shards(): weight_share = lax.psum(weight_share, 'dp')  90.9 us
    add x54, other arithmetic, one_tap(): old_rows + back_sum  41.1 us
    reduce_sum x72, other arithmetic, one_tap(): horiz_rows.append(jnp.sum(scaled * shifted, 0))  29.5 us
    mul x90, other arithmetic, one_tap(): weight_row * scaled  29.4 us
    scatter-add x7, local copies, waits for them, and re-layouts, fold_patches(): folded = folded.at[:, row_shift:row_shift + row_count, col_shift:col_shif...  28.3 us
    reduce_sum x54, other arithmetic, one_tap(): jnp.sum(upstream * blended, 0)[None]  25.7 us
    dynamic_update_slice x54, local copies, waits for them, and re-layouts, one_tap(): lax.dynamic_update_slice_in_dim(grad_padded, old_rows + back_sum, tap_ind...  16.6 us
    dynamic_update_slice x54, local copies, waits for them, and re-layouts, one_tap(): lax.dynamic_update_slice_in_dim(grad_vert, jnp.sum(upstream * blended, 0)...  16.3 us
  transfers between devices with their start and end apart: 10, of which 5 were waited for; matrix products, arithmetic and copies ran while one was open for 2% of the time, Pallas kernels for 0%

commit v1 on v0

v1 whole, which is shorter than its diff:
```python
import functools

import jax
import jax.numpy as jnp
from jax import lax
from jax.experimental import pallas as pl
from jax.experimental.pallas import tpu as pltpu
from jax.sharding import PartitionSpec as P

F32 = jnp.float32
BF16 = jnp.bfloat16
NN = (((1,), (0,)), ((), ()))
NT = (((1,), (1,)), ((), ()))
TN = (((0,), (0,)), ((), ()))


def mm(lhs, rhs, dims):
    return lax.dot_general(lhs, rhs, dims, preferred_element_type=F32)


def halves(value):
    high = value.astype(BF16)
    return high, (value - high.astype(F32)).astype(BF16)


def forward_front(tap_count):
    return -((tap_count - 1) // 2) % 8


def mirror_front(tap_count, cols):
    return (cols - 1 - (tap_count - 1) // 2) % 8


def skew(value, shift):
    count, cols = value.shape
    return jnp.concatenate(
        [
            pltpu.roll(value[row : row + 8], (shift + row) % cols, 1, stride=1, stride_axis=0)
            for row in range(0, count, 8)
        ],
        0,
    )


def local_kernel(
    tap_count,
    feat_ref,
    frame_ref,
    g_ref,
    w_ref,
    wt_ref,
    weight_ref,
    fgrad_ref,
    frim_ref,
    image_ref,
    patch_s,
    kern_s,
    kgrad_s,
    mirror_s,
):
    _, rows, cols = g_ref.shape
    channels = feat_ref.shape[0]
    padded_taps = w_ref.shape[0] // 4
    depth = 3 * channels
    rim = (tap_count - 1) // 2
    scale = tap_count ** (-0.5)
    lane = lax.broadcasted_iota(jnp.int32, (channels, cols), 1)
    first, last = lane == 0, lane == cols - 1

    for row in range(rows + 2):
        at = pl.ds(row * cols, cols)
        piece = feat_ref[:, at]
        wide = piece.astype(F32)
        patch_s[0:channels, at] = jnp.where(first, 0.0, pltpu.roll(wide, 1, 1)).astype(BF16)
        patch_s[channels : 2 * channels, at] = piece
        patch_s[2 * channels : depth, at] = jnp.where(
            last, 0.0, pltpu.roll(wide, cols - 1, 1)
        ).astype(BF16)

    group = 2
    for start in range(0, rows, group):
        stack = jnp.concatenate(
            [patch_s[:, (start + a) * cols : (start + a + group) * cols] for a in range(3)], 0
        )
        kern_s[:, start * cols : (start + group) * cols] = mm(w_ref[...], stack, NN) * scale

    image_ref[...] = jnp.zeros_like(image_ref)
    x_at = lax.broadcasted_iota(jnp.int32, (cols, cols), 0)
    q_at = lax.broadcasted_iota(jnp.int32, (cols, cols), 1)
    band = jnp.abs(q_at - x_at) <= rim
    mirror_band = jnp.abs(cols - 1 - q_at - x_at) <= rim
    in_second = q_at >= 2 * padded_taps
    front = forward_front(tap_count)
    back_shift = mirror_front(tap_count, cols) - (cols + rim - tap_count)

    mirror = jnp.where(q_at + x_at == cols - 1, 1.0, 0.0).astype(BF16)
    for f in range(2):
        for c in range(3):
            mirror_s[f, c] = mm(frame_ref[f, c].astype(BF16), mirror, NN)

    for y in range(rows):
        at = pl.ds(y * cols, cols)
        kern = kern_s[:, at]
        kern_t = jnp.transpose(kern)
        g_rows = [g_ref[c, y : y + 1, :] for c in range(3)]
        vert_parts, horiz_parts = [], []
        for f in range(2):
            base = (2 * f + 1) * padded_taps
            skewed = jnp.where(band, skew(kern_t, -(base + front + rim)), 0.0)
            k_high, k_low = halves(skewed)
            window, mirrored = [
                jnp.concatenate(
                    [ref[f, c, y : y + padded_taps, :] for c in range(3)], 0
                ).astype(BF16)
                for ref in (frame_ref, mirror_s)
            ]
            blend = mm(
                jnp.concatenate([window, window], 1), jnp.concatenate([k_high, k_low], 1), NT
            )
            grad_vert = g_rows[0] * blend[0:padded_taps]
            for c in range(1, 3):
                grad_vert += g_rows[c] * blend[c * padded_taps : (c + 1) * padded_taps]
            vert_parts.append(grad_vert)
            vertical = kern[2 * f * padded_taps : (2 * f + 1) * padded_taps]
            vg_high, vg_low = halves(jnp.concatenate([vertical * g for g in g_rows], 0))
            back = mm(
                jnp.concatenate([vg_high, vg_high], 1), jnp.concatenate([k_high, k_low], 0), NN
            )
            for c in range(3):
                image_ref[f, c, y : y + padded_taps, :] += back[
                    c * padded_taps : (c + 1) * padded_taps
                ]
            cross = mm(
                jnp.concatenate([vg_high, vg_low], 0), jnp.concatenate([mirrored, mirrored], 0), TN
            )
            horiz_parts.append(skew(jnp.where(mirror_band, cross, 0.0), base + back_shift))
        horiz = jnp.transpose(jnp.where(in_second, horiz_parts[1], horiz_parts[0]))
        kgrad_s[:, at] = (
            jnp.concatenate(
                [
                    vert_parts[0],
                    horiz[padded_taps : 2 * padded_taps],
                    vert_parts[1],
                    horiz[3 * padded_taps : 4 * padded_taps],
                ],
                0,
            )
            * scale
        ).astype(BF16)

    for a in range(3):
        part = mm(kgrad_s[...], patch_s[:, a * cols : (a + rows) * cols], NT)
        weight_ref[a] = part

    for row in range(rows + 2):
        total = None
        for a in range(3):
            y = row - a
            if 0 <= y < rows:
                term = mm(
                    wt_ref[a * depth : (a + 1) * depth, :], kgrad_s[:, y * cols : (y + 1) * cols], NN
                )
                total = term if total is None else total + term
        left = total[0:channels]
        right = total[2 * channels : depth]
        result = (
            jnp.where(last, 0.0, pltpu.roll(left, cols - 1, 1))
            + total[channels : 2 * channels]
            + jnp.where(first, 0.0, pltpu.roll(right, 1, 1))
        )
        if row == 0:
            frim_ref[0] = result
        elif row == rows + 1:
            frim_ref[1] = result
        else:
            fgrad_ref[:, row - 1, :] = result


def local_grads(feature_flat, frame_wide, upstream, padded_weight, mirror_weight, tap_count):
    _, rows, cols = upstream.shape
    channels = feature_flat.shape[0]
    outs = padded_weight.shape[0]
    vmem = pl.BlockSpec(memory_space=pltpu.VMEM)
    return pl.pallas_call(
        functools.partial(local_kernel, tap_count),
        out_shape=[
            jax.ShapeDtypeStruct((3, outs, 3 * channels), F32),
            jax.ShapeDtypeStruct((channels, rows, cols), F32),
            jax.ShapeDtypeStruct((2, channels, cols), F32),
            jax.ShapeDtypeStruct(frame_wide.shape, F32),
        ],
        in_specs=[vmem] * 5,
        out_specs=[vmem] * 4,
        scratch_shapes=[
            pltpu.VMEM((3 * channels, (rows + 2) * cols), BF16),
            pltpu.VMEM((outs, rows * cols), F32),
            pltpu.VMEM((outs, rows * cols), BF16),
            pltpu.VMEM(frame_wide.shape, F32),
        ],
        compiler_params=pltpu.CompilerParams(vmem_limit_bytes=40 * 1024 * 1024),
    )(feature_flat, frame_wide, upstream, padded_weight, mirror_weight.T)


def both_ways(head, tail, axis):
    count = lax.axis_size(axis)
    ends = count - 1
    before = lax.ppermute(tail, axis, [(i, i + 1) for i in range(ends)])
    after = lax.ppermute(head, axis, [(i + 1, i) for i in range(ends)])
    return before, after


def shards(frames, features, cotangent, head_weight):
    taps = head_weight.shape[0] // 4
    padded_taps = -(-taps // 32) * 32
    rim = (taps - 1) // 2
    feature_map = features[0]
    channels, rows, cols = feature_map.shape
    image = frames[0]
    upstream = cotangent[0]
    lead = image.shape[:2]

    def packed(rim_rows, row):
        return jnp.concatenate([rim_rows.reshape(-1, cols), row.reshape(-1, cols)], 0)

    def unpacked(value):
        split = lead[0] * lead[1] * rim
        return value[:split].reshape(lead + (rim, cols)), value[split:].reshape(channels, 1, cols)

    before, after = both_ways(
        packed(image[:, :, :rim], feature_map[:, :1]),
        packed(image[:, :, rows - rim :], feature_map[:, rows - 1 :]),
        "tile",
    )
    image_before, row_before = unpacked(before)
    image_after, row_after = unpacked(after)
    extra = -(rows + 2 * rim) % 8
    extra += 0 if rows + 2 * rim + extra >= rows + padded_taps - 1 else 8
    frame_wide = jnp.concatenate(
        [image_before, image, image_after, jnp.zeros(lead + (extra, cols), BF16)], 2
    ).astype(F32)
    feature_flat = jnp.concatenate([row_before, feature_map, row_after], 1).reshape(
        channels, (rows + 2) * cols
    )
    by_group = head_weight.reshape(2, 2, taps, -1)

    def in_groups(vertical, horizontal, front):
        gap = padded_taps - taps
        return jnp.concatenate(
            [
                jnp.pad(vertical[:, None], ((0, 0), (0, 0), (0, gap), (0, 0))),
                jnp.pad(horizontal[:, None], ((0, 0), (0, 0), (front, gap - front), (0, 0))),
            ],
            1,
        ).reshape(4 * padded_taps, -1)

    back_front = mirror_front(taps, cols)
    padded_weight = in_groups(by_group[:, 0], by_group[:, 1], forward_front(taps))
    mirror_weight = in_groups(by_group[:, 0], by_group[:, 1, ::-1], back_front)

    weight_parts, feat_mid, feat_rims, image_grad = local_grads(
        feature_flat, frame_wide, upstream, padded_weight, mirror_weight, taps
    )
    before, after = both_ways(
        packed(image_grad[:, :, :rim], feat_rims[0]),
        packed(image_grad[:, :, rows + rim : rows + 2 * rim], feat_rims[1]),
        "tile",
    )
    image_before, row_before = unpacked(before)
    image_after, row_after = unpacked(after)
    middle = image_grad[:, :, rim : rim + rows]
    middle = middle.at[:, :, :rim].add(image_before).at[:, :, rows - rim :].add(image_after)
    feat_grad = jnp.concatenate(
        [feat_mid[:, :1] + row_before, feat_mid[:, 1 : rows - 1], feat_mid[:, rows - 1 :] + row_after], 1
    )

    weight_part = weight_parts
    for axis in ("dp", "tile"):
        count = lax.axis_size(axis)
        step = 1
        while step < count:
            weight_part = weight_part + lax.ppermute(
                weight_part, axis, [(i, i ^ step) for i in range(count)]
            )
            step *= 2
    weight_sum = weight_part.transpose(1, 0, 2).reshape(2, 2, padded_taps, -1)
    weight_sum = jnp.concatenate(
        [
            weight_sum[:, :1, :taps],
            weight_sum[:, 1:, back_front : back_front + taps][:, :, ::-1],
        ],
        1,
    ).reshape(4 * taps, -1)
    pixel_count = lax.axis_size("dp") * lax.axis_size("tile") * rows * cols
    return (weight_sum * pixel_count ** (-0.5), feat_grad[None], middle[None])


def solution(mesh):
    in_specs = (
        P("dp", None, None, "tile", None),
        P("dp", None, "tile", None),
        P("dp", None, "tile", None),
        P(),
    )
    out_specs = (P(), P("dp", None, "tile", None), P("dp", None, None, "tile", None))
    return jax.shard_map(shards, mesh=mesh, in_specs=in_specs, out_specs=out_specs, check_vma=False)
```

time: 394 us -> 73.6 us (0.19)
  other arithmetic: 143 us -> 1.49 us
  local copies, waits for them, and re-layouts: 87.6 us -> 5.79 us
  waiting for transfers between devices: 102 us -> 39 us
  loops' own time: 14.3 us -> 0 us
  between operations: 14.7 us -> 1 us
  blocking collectives: 6.18 us -> 0 us
  matrix products: 5.03 us -> 0 us
  Pallas kernels: 0 us -> 4.47 us
    psum x1 -> x0, waiting for transfers between devices: 90.9 us -> none  [shards(): weight_share = lax.psum(weight_share, 'dp')]
    reduce_sum x126 -> x0, other arithmetic: 55.2 us -> none  [the longest x72 29.5 us: one_tap(): horiz_rows.append(jnp.sum(scaled * shifted, 0))]
    add x78 -> x6, other arithmetic: 50.4 us -> 0.28 us  [the longest x4 0.2 us: shards(): weight_part + lax.ppermute(weight_part, axis, [(i, i ^ step) for i in ran...]
    ppermute x8 -> x9, waiting for transfers between devices: 4.94 us -> 39 us  [the longest x5 36.1 us: shards(): lax.ppermute(weight_part, axis, [(i, i ^ step) for i in range(count)])]
    dynamic_update_slice x108 -> x0, local copies, waits for them, and re-layouts: 32.9 us -> none  [the longest x54 16.6 us: one_tap(): lax.dynamic_update_slice_in_dim(grad_padded, old_rows + back_sum, tap_ind...]
    mul x92 -> x1, other arithmetic: 29.6 us -> 0.03 us  [shards(): return (weight_sum * pixel_count ** (-0.5), feat_grad[None], middle[None])]
    scatter-add x10 -> x2, local copies, waits for them, and re-layouts: 28.8 us -> 0.33 us  [shards(): middle.at[:, :, :rim].add(image_before).at[:, :, rows - rim:]]
    another operation x2 -> x0, loops' own time: 14.3 us -> none  [separable_grads(): return lax.fori_loop(0, tap_count // group_size, group_step, start_state)]
  transfers between devices with their start and end apart: 10 -> 9, of which waited for: 5 -> 7; matrix products, arithmetic and copies ran while one was open for 2% -> 3% of each run, Pallas kernels for 0% -> 0%
where the time goes in v1:
time: 73.6 us; the launch traced here: 73.2 us
  waiting for transfers between devices  39 us (53%)
  starting transfers between devices  21.4 us (29%)
  local copies, waits for them, and re-layouts  5.79 us (8%)
  Pallas kernels  4.47 us (6%)
  other arithmetic  1.49 us (2%)
  between operations  1 us (1%)
    ppermute x5, waiting for transfers between devices, shards(): lax.ppermute(weight_part, axis, [(i, i ^ step) for i in range(count)])  36.1 us
    ppermute x5, starting transfers between devices, shards(): lax.ppermute(weight_part, axis, [(i, i ^ step) for i in range(count)])  9.62 us
    ppermute x2, starting transfers between devices, both_ways(): before = lax.ppermute(tail, axis, [(i, i + 1) for i in range(ends)])  9.08 us
    pallas_call x1, Pallas kernels, local_grads(): pl.pallas_call(functools.partial(local_kernel, tap_count), out_shape=[jax...  4.47 us
    ppermute x2, waiting for transfers between devices, both_ways(): before = lax.ppermute(tail, axis, [(i, i + 1) for i in range(ends)])  2.9 us
    ppermute x2, starting transfers between devices, both_ways(): after = lax.ppermute(head, axis, [(i + 1, i) for i in range(ends)])  2.72 us
    unnamed x9, local copies, waits for them, and re-layouts  2.38 us
  transfers between devices with their start and end apart: 9, of which 7 were waited for; matrix products, arithmetic and copies ran while one was open for 3% of the time, Pallas kernels for 0%

profile of v1, /device:TPU:0, one launch (start us, length us, event | category | flops | bytes accessed | tf_op | source)
XLA Modules:
  0.0 73.2 jit_solution(8391240668351207546)
XLA Ops:
  0.6 0.8 %fusion.8 = (bf16[2,3,13,128]{3,2,1,0:T(8,128)(2,1)S(1)}, bf16[2,3,13,128]{3,2,1,0:T(8,128)(2,1)S(1)}) fusion(bf16[2,3,16,128]{3,2,1,0:T(8,128)(2,1)} %bitcast.40), kind=kLoop, calls=%fused_computation.31 | loop fusion | bytes 79872 | tf_op jit(solution)/shard_map/slice | solution.py:231
  1.5 1.0 %copy.19 = bf16[1,64,16,128]{3,1,2,0:T(8,128)(2,1)S(1)} copy(bf16[1,64,16,128]{3,2,1,0:T(8,128)(2,1)} %param.9) | data formatting | bytes 524288 | tf_op args[1]
  2.5 0.0 copy-start.3
  2.5 1.4 %collective-permute-start.1 = (bf16[142,128]{1,0:T(8,128)(2,1)S(1)}, bf16[142,128]{1,0:T(8,128)(2,1)S(1)}, u32[]{:S(2)}, u32[]{:S(2)}) collective-permute-start(bf16[142,128]{1,0:T(8,128)(2,1)S(1)} %pad_maximum_fusion.3), channel_id=1, source_target_pairs={{1,0},{3,2},{5,4},{7,6},{9,8},{11,10},{13,12},{15,14},{17,16},{19,... | collective-permute-start | bytes 109064 | tf_op jit(solution)/shard_map/ppermute | solution.py:208
  4.0 4.8 %collective-permute-start = (bf16[142,128]{1,0:T(8,128)(2,1)S(1)}, bf16[142,128]{1,0:T(8,128)(2,1)S(1)}, u32[]{:S(2)}, u32[]{:S(2)}) collective-permute-start(bf16[142,128]{1,0:T(8,128)(2,1)S(1)} %pad_maximum_fusion.2), channel_id=1, source_target_pairs={{0,1},{2,3},{4,5},{6,7},{8,9},{10,11},{12,13},{14,15},{16,17},{18,... | collective-permute-start | bytes 109064 | tf_op jit(solution)/shard_map/ppermute | solution.py:207
  8.9 0.0 copy-done.3
  8.9 0.1 reshape.147
  9.0 0.2 rev.6
  9.2 0.1 fusion.4
  9.3 0.1 copy.14
  9.4 0.1 pad.36.clone
  9.5 0.0 collective-permute-done.1
  9.6 0.9 %collective-permute-done = bf16[142,128]{1,0:T(8,128)(2,1)S(1)} collective-permute-done((bf16[142,128]{1,0:T(8,128)(2,1)S(1)}, bf16[142,128]{1,0:T(8,128)(2,1)S(1)}, u32[]{:S(2)}, u32[]{:S(2)}) %collective-permute-start) | collective-permute-done | bytes 36384 | tf_op jit(solution)/shard_map/ppermute | solution.py:207
  10.6 0.0 copy-start.1
  10.6 0.7 copy-done.1
  11.3 0.0 copy-start
  11.3 0.1 maximum_convert_fusion.frame_ref
  11.4 0.7 copy-done
  12.0 4.5 %shard_map.67 = (f32[3,128,192]{2,1,0:T(8,128)S(1)}, f32[64,16,128]{2,1,0:T(8,128)S(1)}, f32[2,64,128]{2,1,0:T(8,128)S(1)}, f32[2,3,48,128]{3,2,1,0:T(8,128)S(1)}) custom-call(bf16[64,2304]{1,0:T(8,128)(2,1)S(1)} %copy_bitcast_fusion.feat_ref, f32[2,3,48,128]{3,2,1,0:T(8,128)S(1)} %maximum_convert_fusion.frame_ref, f32[3,16,128]{2,1,0:T(8,128)S(1)} %bitcast.36, ...), custom_call_target="tpu_custom_call" | custom-call | tf_op jit(solution)/shard_map/pallas_call | solution.py:184
  16.5 0.1 collective-permute-start.2
  16.6 1.7 %collective-permute-done.2 = f32[3,128,192]{2,1,0:T(8,128)S(1)} collective-permute-done((f32[3,128,192]{2,1,0:T(8,128)S(1)}, f32[3,128,192]{2,1,0:T(8,128)S(1)}, u32[]{:S(2)}, u32[]{:S(2)}) %collective-permute-start.2) | collective-permute-done | bytes 294944 | tf_op jit(solution)/shard_map/ppermute | solution.py:281
  18.3 0.1 add.41
  18.4 2.7 %collective-permute-start.3 = (f32[3,128,192]{2,1,0:T(8,128)S(1)}, f32[3,128,192]{2,1,0:T(8,128)S(1)}, u32[]{:S(2)}, u32[]{:S(2)}) collective-permute-start(f32[3,128,192]{2,1,0:T(8,128)S(1)} %add.41), channel_id=1, source_target_pairs={{0,4},{2,6},{4,0},{6,2},{8,12},{10,14},{12,8},{14,10},{16,20},{18,... | collective-permute-start | bytes 884744 | tf_op jit(solution)/shard_map/ppermute | solution.py:281
  21.1 4.2 %collective-permute-start.7 = (f32[142,128]{1,0:T(8,128)S(1)}, f32[142,128]{1,0:T(8,128)S(1)}, u32[]{:S(2)}, u32[]{:S(2)}) collective-permute-start(f32[142,128]{1,0:T(8,128)S(1)} %pad_maximum_fusion), channel_id=1, source_target_pairs={{0,1},{2,3},{4,5},{6,7},{8,9},{10,11},{12,13},{14,15},{16,17},{18,... | collective-permute-start | bytes 218120 | tf_op jit(solution)/shard_map/ppermute | solution.py:207
  25.4 2.0 %collective-permute-done.7 = f32[142,128]{1,0:T(8,128)S(1)} collective-permute-done((f32[142,128]{1,0:T(8,128)S(1)}, f32[142,128]{1,0:T(8,128)S(1)}, u32[]{:S(2)}, u32[]{:S(2)}) %collective-permute-start.7) | collective-permute-done | bytes 72736 | tf_op jit(solution)/shard_map/ppermute | solution.py:207
  27.4 3.2 %collective-permute-done.3 = f32[3,128,192]{2,1,0:T(8,128)S(1)} collective-permute-done((f32[3,128,192]{2,1,0:T(8,128)S(1)}, f32[3,128,192]{2,1,0:T(8,128)S(1)}, u32[]{:S(2)}, u32[]{:S(2)}) %collective-permute-start.3) | collective-permute-done | bytes 294944 | tf_op jit(solution)/shard_map/ppermute | solution.py:281
  30.5 0.1 add.42
  30.6 1.9 %collective-permute-start.4 = (f32[3,128,192]{2,1,0:T(8,128)S(1)}, f32[3,128,192]{2,1,0:T(8,128)S(1)}, u32[]{:S(2)}, u32[]{:S(2)}) collective-permute-start(f32[3,128,192]{2,1,0:T(8,128)S(1)} %add.42), channel_id=1, source_target_pairs={{0,8},{2,10},{4,12},{6,14},{8,0},{10,2},{12,4},{14,6},{16,24},{18,... | collective-permute-start | bytes 884744 | tf_op jit(solution)/shard_map/ppermute | solution.py:281
  32.5 1.3 %collective-permute-start.8 = (f32[142,128]{1,0:T(8,128)S(1)}, f32[142,128]{1,0:T(8,128)S(1)}, u32[]{:S(2)}, u32[]{:S(2)}) collective-permute-start(f32[142,128]{1,0:T(8,128)S(1)} %pad_maximum_fusion.1), channel_id=1, source_target_pairs={{1,0},{3,2},{5,4},{7,6},{9,8},{11,10},{13,12},{15,14},{17,16},{19,... | collective-permute-start | bytes 218120 | tf_op jit(solution)/shard_map/ppermute | solution.py:208
  33.8 7.5 %collective-permute-done.4 = f32[3,128,192]{2,1,0:T(8,128)S(1)} collective-permute-done((f32[3,128,192]{2,1,0:T(8,128)S(1)}, f32[3,128,192]{2,1,0:T(8,128)S(1)}, u32[]{:S(2)}, u32[]{:S(2)}) %collective-permute-start.4) | collective-permute-done | bytes 294944 | tf_op jit(solution)/shard_map/ppermute | solution.py:281
  41.3 0.1 add.43
  41.3 2.6 %collective-permute-start.5 = (f32[3,128,192]{2,1,0:T(8,128)S(1)}, f32[3,128,192]{2,1,0:T(8,128)S(1)}, u32[]{:S(2)}, u32[]{:S(2)}) collective-permute-start(f32[3,128,192]{2,1,0:T(8,128)S(1)} %add.43), channel_id=1, source_target_pairs={{0,16},{2,18},{4,20},{6,22},{8,24},{10,26},{12,28},{14,30},{16,0},... | collective-permute-start | bytes 884744 | tf_op jit(solution)/shard_map/ppermute | solution.py:281
  43.9 0.2 scatter-add.6
  44.1 0.0 collective-permute-done.8
  44.2 0.2 scatter-add.9
  44.3 0.0 copy-start.2
  44.4 16.1 %collective-permute-done.5 = f32[3,128,192]{2,1,0:T(8,128)S(1)} collective-permute-done((f32[3,128,192]{2,1,0:T(8,128)S(1)}, f32[3,128,192]{2,1,0:T(8,128)S(1)}, u32[]{:S(2)}, u32[]{:S(2)}) %collective-permute-start.5) | collective-permute-done | bytes 294944 | tf_op jit(solution)/shard_map/ppermute | solution.py:281
  60.5 0.1 add.44
  60.5 0.0 copy-done.2
  60.5 2.4 %collective-permute-start.6 = (f32[3,128,192]{2,1,0:T(8,128)S(1)}, f32[3,128,192]{2,1,0:T(8,128)S(1)}, u32[]{:S(2)}, u32[]{:S(2)}) collective-permute-start(f32[3,128,192]{2,1,0:T(8,128)S(1)} %add.44), channel_id=1, source_target_pairs={{0,1},{1,0},{2,3},{3,2},{4,5},{5,4},{6,7},{7,6},{8,9},{9,8},{10,11... | collective-permute-start | bytes 884744 | tf_op jit(solution)/shard_map/ppermute | solution.py:281
  62.9 0.1 slice_add_fusion.3
  63.0 0.9 %maximum_bitcast_fusion = f32[1,64,16,128]{3,2,1,0:T(8,128)} fusion(f32[64,1,128]{2,1,0:T(1,128)S(1)} %get-tuple-element.36, f32[64,14,128]{2,1,0:T(8,128)S(1)} %slice.149, f32[64,1,128]{2,1,0:T(1,128)S(1)} %get-tuple-element.35), kind=kLoop, calls=%fused_computation | loop fusion | flops 262144 | bytes 1048576 | tf_op jit(solution)/shard_map/broadcast_in_dim | solution.py:294
  63.9 7.7 %collective-permute-done.6 = f32[3,128,192]{2,1,0:T(8,128)S(1)} collective-permute-done((f32[3,128,192]{2,1,0:T(8,128)S(1)}, f32[3,128,192]{2,1,0:T(8,128)S(1)}, u32[]{:S(2)}, u32[]{:S(2)}) %collective-permute-start.6) | collective-permute-done | bytes 294944 | tf_op jit(solution)/shard_map/ppermute | solution.py:281
  71.6 0.1 add_bitcast_fusion
  71.6 0.3 copy.15
  71.9 0.3 reshape.150
  72.2 0.2 rev.7
  72.5 0.7 %mul.11 = f32[108,576]{1,0:T(8,128)} reshape(f32[2,2,27,576]{3,2,1,0:T(8,128)S(1)} %maximum_multiply_fusion) | data formatting | bytes 497664 | tf_op jit(solution)/shard_map/mul | solution.py:294
  (32 shorter events, 0.4 us)
Async XLA Ops:
  2.5 6.4 %copy-start.3 = (bf16[108,576]{1,0:T(8,128)(2,1)S(1)}, bf16[108,576]{1,0:T(8,128)(2,1)}, u32[]{:S(2)}) copy-start(bf16[108,576]{1,0:T(8,128)(2,1)} %param.11) | copy-start | bytes 373252
  2.5 7.0 %collective-permute-start.1 = (bf16[142,128]{1,0:T(8,128)(2,1)S(1)}, bf16[142,128]{1,0:T(8,128)(2,1)S(1)}, u32[]{:S(2)}, u32[]{:S(2)}) collective-permute-start(bf16[142,128]{1,0:T(8,128)(2,1)S(1)} %pad_maximum_fusion.3), channel_id=1, source_target_pairs={{1,0},{3,2},{5,4},{7,6},{9,8},{11,10},{13,12},{15,14},{17,16},{19,... | collective-permute-start | bytes 109064 | tf_op jit(solution)/shard_map/ppermute | solution.py:208
  4.0 6.5 %collective-permute-start = (bf16[142,128]{1,0:T(8,128)(2,1)S(1)}, bf16[142,128]{1,0:T(8,128)(2,1)S(1)}, u32[]{:S(2)}, u32[]{:S(2)}) collective-permute-start(bf16[142,128]{1,0:T(8,128)(2,1)S(1)} %pad_maximum_fusion.2), channel_id=1, source_target_pairs={{0,1},{2,3},{4,5},{6,7},{8,9},{10,11},{12,13},{14,15},{16,17},{18,... | collective-permute-start | bytes 109064 | tf_op jit(solution)/shard_map/ppermute | solution.py:207
  10.6 0.7 %copy-start.1 = (bf16[1,2,3,16,128]{4,3,2,1,0:T(8,128)(2,1)S(1)}, bf16[1,2,3,16,128]{4,3,2,1,0:T(8,128)(2,1)}, u32[]{:S(2)}) copy-start(bf16[1,2,3,16,128]{4,3,2,1,0:T(8,128)(2,1)} %param.8) | copy-start | bytes 73732
  11.3 0.7 %copy-start = (f32[1,3,16,128]{3,2,1,0:T(8,128)S(1)}, f32[1,3,16,128]{3,2,1,0:T(8,128)}, u32[]{:S(2)}) copy-start(f32[1,3,16,128]{3,2,1,0:T(8,128)} %param.10) | copy-start | bytes 73732
  16.5 1.8 %collective-permute-start.2 = (f32[3,128,192]{2,1,0:T(8,128)S(1)}, f32[3,128,192]{2,1,0:T(8,128)S(1)}, u32[]{:S(2)}, u32[]{:S(2)}) collective-permute-start(f32[3,128,192]{2,1,0:T(8,128)S(1)} %get-tuple-element.31), channel_id=1, source_target_pairs={{0,2},{2,0},{4,6},{6,4},{8,10},{10,8},{12,14},{14,12},{16,18},{18,... | collective-permute-start | bytes 884744 | tf_op jit(solution)/shard_map/ppermute | solution.py:281
  18.4 12.2 %collective-permute-start.3 = (f32[3,128,192]{2,1,0:T(8,128)S(1)}, f32[3,128,192]{2,1,0:T(8,128)S(1)}, u32[]{:S(2)}, u32[]{:S(2)}) collective-permute-start(f32[3,128,192]{2,1,0:T(8,128)S(1)} %add.41), channel_id=1, source_target_pairs={{0,4},{2,6},{4,0},{6,2},{8,12},{10,14},{12,8},{14,10},{16,20},{18,... | collective-permute-start | bytes 884744 | tf_op jit(solution)/shard_map/ppermute | solution.py:281
  21.1 6.2 %collective-permute-start.7 = (f32[142,128]{1,0:T(8,128)S(1)}, f32[142,128]{1,0:T(8,128)S(1)}, u32[]{:S(2)}, u32[]{:S(2)}) collective-permute-start(f32[142,128]{1,0:T(8,128)S(1)} %pad_maximum_fusion), channel_id=1, source_target_pairs={{0,1},{2,3},{4,5},{6,7},{8,9},{10,11},{12,13},{14,15},{16,17},{18,... | collective-permute-start | bytes 218120 | tf_op jit(solution)/shard_map/ppermute | solution.py:207
  30.6 10.7 %collective-permute-start.4 = (f32[3,128,192]{2,1,0:T(8,128)S(1)}, f32[3,128,192]{2,1,0:T(8,128)S(1)}, u32[]{:S(2)}, u32[]{:S(2)}) collective-permute-start(f32[3,128,192]{2,1,0:T(8,128)S(1)} %add.42), channel_id=1, source_target_pairs={{0,8},{2,10},{4,12},{6,14},{8,0},{10,2},{12,4},{14,6},{16,24},{18,... | collective-permute-start | bytes 884744 | tf_op jit(solution)/shard_map/ppermute | solution.py:281
  32.5 11.6 %collective-permute-start.8 = (f32[142,128]{1,0:T(8,128)S(1)}, f32[142,128]{1,0:T(8,128)S(1)}, u32[]{:S(2)}, u32[]{:S(2)}) collective-permute-start(f32[142,128]{1,0:T(8,128)S(1)} %pad_maximum_fusion.1), channel_id=1, source_target_pairs={{1,0},{3,2},{5,4},{7,6},{9,8},{11,10},{13,12},{15,14},{17,16},{19,... | collective-permute-start | bytes 218120 | tf_op jit(solution)/shard_map/ppermute | solution.py:208
  41.3 19.1 %collective-permute-start.5 = (f32[3,128,192]{2,1,0:T(8,128)S(1)}, f32[3,128,192]{2,1,0:T(8,128)S(1)}, u32[]{:S(2)}, u32[]{:S(2)}) collective-permute-start(f32[3,128,192]{2,1,0:T(8,128)S(1)} %add.43), channel_id=1, source_target_pairs={{0,16},{2,18},{4,20},{6,22},{8,24},{10,26},{12,28},{14,30},{16,0},... | collective-permute-start | bytes 884744 | tf_op jit(solution)/shard_map/ppermute | solution.py:281
  44.3 16.2 %copy-start.2 = (f32[1,2,3,16,128]{4,3,2,1,0:T(8,128)}, f32[1,2,3,16,128]{4,3,2,1,0:T(8,128)S(1)}, u32[]{:S(2)}) copy-start(f32[1,2,3,16,128]{4,3,2,1,0:T(8,128)S(1)} %scatter-add.9) | copy-start | bytes 147460
  60.5 11.1 %collective-permute-start.6 = (f32[3,128,192]{2,1,0:T(8,128)S(1)}, f32[3,128,192]{2,1,0:T(8,128)S(1)}, u32[]{:S(2)}, u32[]{:S(2)}) collective-permute-start(f32[3,128,192]{2,1,0:T(8,128)S(1)} %add.44), channel_id=1, source_target_pairs={{0,1},{1,0},{2,3},{3,2},{4,5},{5,4},{6,7},{7,6},{8,9},{9,8},{10,11... | collective-permute-start | bytes 884744 | tf_op jit(solution)/shard_map/ppermute | solution.py:281

commit v2 on v1

--- a/solution.py
+++ b/solution.py
@@ -29,6 +29,18 @@
 
 def mirror_front(tap_count, cols):
     return (cols - 1 - (tap_count - 1) // 2) % 8
+
+
+def natural_order(tap_count, padded_taps, cols):
+    size = 4 * padded_taps
+    out_at = lax.broadcasted_iota(jnp.int32, (size, size), 0)
+    in_at = lax.broadcasted_iota(jnp.int32, (size, size), 1)
+    chosen = jnp.full((size, size), -1, jnp.int32)
+    for group in range(4):
+        tap = out_at - group * tap_count
+        place = tap if group % 2 == 0 else mirror_front(tap_count, cols) + tap_count - 1 - tap
+        chosen = jnp.where((tap >= 0) & (tap < tap_count), group * padded_taps + place, chosen)
+    return jnp.where(chosen == in_at, 1.0, 0.0).astype(BF16)
 
 
 def skew(value, shift):
@@ -51,12 +63,13 @@
     wt_ref,
     weight_ref,
     fgrad_ref,
-    frim_ref,
+    rims_ref,
     image_ref,
     patch_s,
     kern_s,
     kgrad_s,
     mirror_s,
+    image_s,
 ):
     _, rows, cols = g_ref.shape
     channels = feat_ref.shape[0]
@@ -84,10 +97,11 @@
         )
         kern_s[:, start * cols : (start + group) * cols] = mm(w_ref[...], stack, NN) * scale
 
-    image_ref[...] = jnp.zeros_like(image_ref)
+    image_s[...] = jnp.zeros_like(image_s)
     x_at = lax.broadcasted_iota(jnp.int32, (cols, cols), 0)
     q_at = lax.broadcasted_iota(jnp.int32, (cols, cols), 1)
     band = jnp.abs(q_at - x_at) <= rim
+    natural = natural_order(tap_count, padded_taps, cols)
     mirror_band = jnp.abs(cols - 1 - q_at - x_at) <= rim
     in_second = q_at >= 2 * padded_taps
     front = forward_front(tap_count)
@@ -127,7 +141,7 @@
                 jnp.concatenate([vg_high, vg_high], 1), jnp.concatenate([k_high, k_low], 0), NN
             )
             for c in range(3):
-                image_ref[f, c, y : y + padded_taps, :] += back[
+                image_s[f, c, y : y + padded_taps, :] += back[
                     c * padded_taps : (c + 1) * padded_taps
                 ]
             cross = mm(
@@ -135,22 +149,21 @@
             )
             horiz_parts.append(skew(jnp.where(mirror_band, cross, 0.0), base + back_shift))
         horiz = jnp.transpose(jnp.where(in_second, horiz_parts[1], horiz_parts[0]))
-        kgrad_s[:, at] = (
-            jnp.concatenate(
-                [
-                    vert_parts[0],
-                    horiz[padded_taps : 2 * padded_taps],
-                    vert_parts[1],
-                    horiz[3 * padded_taps : 4 * padded_taps],
-                ],
-                0,
-            )
-            * scale
-        ).astype(BF16)
+        stacked = jnp.concatenate(
+            [
+                vert_parts[0],
+                horiz[padded_taps : 2 * padded_taps],
+                vert_parts[1],
+                horiz[3 * padded_taps : 4 * padded_taps],
+            ],
+            0,
+        )
+        kgrad_s[:, at] = mm(natural, (stacked * scale).astype(BF16), NN).astype(BF16)
 
     for a in range(3):
-        part = mm(kgrad_s[...], patch_s[:, a * cols : (a + rows) * cols], NT)
-        weight_ref[a] = part
+        weight_ref[a * depth : (a + 1) * depth, :] = mm(
+            patch_s[:, a * cols : (a + rows) * cols], kgrad_s[...], NT
+        )
 
     for row in range(rows + 2):
         total = None
@@ -169,14 +182,24 @@
             + jnp.where(first, 0.0, pltpu.roll(right, 1, 1))
         )
         if row == 0:
-            frim_ref[0] = result
+            rims_ref[0, 0:channels] = result
         elif row == rows + 1:
-            frim_ref[1] = result
+            rims_ref[1, 0:channels] = result
         else:
             fgrad_ref[:, row - 1, :] = result
 
-
-def local_grads(feature_flat, frame_wide, upstream, padded_weight, mirror_weight, tap_count):
+    for f in range(2):
+        for c in range(3):
+            start = channels + (3 * f + c) * rim
+            rims_ref[0, start : start + rim] = image_s[f, c, 0:rim]
+            rims_ref[1, start : start + rim] = image_s[f, c, rows + rim : rows + 2 * rim]
+            image_ref[f, c] = image_s[f, c, rim : rows + rim]
+    spare = channels + 6 * rim
+    if spare < rims_ref.shape[1]:
+        rims_ref[:, spare:] = jnp.zeros((2, rims_ref.shape[1] - spare, cols), F32)
+
+
+def local_grads(feature_flat, frame_wide, upstream, padded_weight, flipped_weight, tap_count, rim_size):
     _, rows, cols = upstream.shape
     channels = feature_flat.shape[0]
     outs = padded_weight.shape[0]
@@ -184,10 +207,10 @@
     return pl.pallas_call(
         functools.partial(local_kernel, tap_count),
         out_shape=[
-            jax.ShapeDtypeStruct((3, outs, 3 * channels), F32),
+            jax.ShapeDtypeStruct((9 * channels, outs), F32),
             jax.ShapeDtypeStruct((channels, rows, cols), F32),
-            jax.ShapeDtypeStruct((2, channels, cols), F32),
-            jax.ShapeDtypeStruct(frame_wide.shape, F32),
+            jax.ShapeDtypeStruct((2, rim_size, cols), F32),
+            jax.ShapeDtypeStruct((2, 3, rows, cols), F32),
         ],
         in_specs=[vmem] * 5,
         out_specs=[vmem] * 4,
@@ -196,17 +219,209 @@
             pltpu.VMEM((outs, rows * cols), F32),
             pltpu.VMEM((outs, rows * cols), BF16),
             pltpu.VMEM(frame_wide.shape, F32),
+            pltpu.VMEM(frame_wide.shape, F32),
         ],
         compiler_params=pltpu.CompilerParams(vmem_limit_bytes=40 * 1024 * 1024),
-    )(feature_flat, frame_wide, upstream, padded_weight, mirror_weight.T)
-
-
-def both_ways(head, tail, axis):
-    count = lax.axis_size(axis)
-    ends = count - 1
-    before = lax.ppermute(tail, axis, [(i, i + 1) for i in range(ends)])
-    after = lax.ppermute(head, axis, [(i + 1, i) for i in range(ends)])
-    return before, after
+    )(feature_flat, frame_wide, upstream, padded_weight, flipped_weight)
+
+
+def greet(peers):
+    barrier = pltpu.get_barrier_semaphore()
+    for peer in peers:
+        pl.semaphore_signal(barrier, inc=1, device_id=peer, device_id_type=pl.DeviceIdType.MESH)
+    pl.semaphore_wait(barrier, len(peers))
+
+
+def push(source, target, send_sem, recv_sem, peer):
+    return pltpu.make_async_remote_copy(
+        src_ref=source,
+        dst_ref=target,
+        send_sem=send_sem,
+        recv_sem=recv_sem,
+        device_id=peer,
+        device_id_type=pl.DeviceIdType.MESH,
+    )
+
+
+class Neighbours:
+    def __init__(self, count, rims_ref, landed, send_sems, recv_sems):
+        dp, tile = lax.axis_index("dp"), lax.axis_index("tile")
+        self.has = (tile > 0, tile < count - 1)
+        peers = ((dp, lax.max(tile - 1, 0)), (dp, lax.min(tile + 1, count - 1)))
+        self.peers, self.landed = peers, landed
+        self.out = [
+            push(rims_ref.at[side], landed.at[1 - side], send_sems.at[side], recv_sems.at[1 - side], peers[side])
+            for side in range(2)
+        ]
+        self.into = [
+            push(rims_ref.at[side], landed.at[side], send_sems.at[side], recv_sems.at[side], peers[side])
+            for side in range(2)
+        ]
+
+    def start(self):
+        for side in range(2):
+            pl.when(self.has[side])(self.out[side].start)
+
+    def finish(self, out_ref):
+        for side in range(2):
+
+            @pl.when(self.has[side])
+            def _():
+                self.into[side].wait_recv()
+                out_ref[side] = self.landed[side]
+                self.out[side].wait_send()
+
+            @pl.when(jnp.logical_not(self.has[side]))
+            def _():
+                out_ref[side] = jnp.zeros(out_ref.shape[1:], out_ref.dtype)
+
+
+def halo_kernel(count, rims_ref, out_ref, landed, send_sems, recv_sems):
+    near = Neighbours(count, rims_ref, landed, send_sems, recv_sems)
+    barrier = pltpu.get_barrier_semaphore()
+    for side in range(2):
+
+        @pl.when(near.has[side])
+        def _():
+            pl.semaphore_signal(
+                barrier, inc=1, device_id=near.peers[side], device_id_type=pl.DeviceIdType.MESH
+            )
+
+    pl.semaphore_wait(barrier, sum(has.astype(jnp.int32) for has in near.has))
+    near.start()
+    near.finish(out_ref)
+
+
+def exchange_halo(rims):
+    vmem = pl.BlockSpec(memory_space=pltpu.VMEM)
+    return pl.pallas_call(
+        functools.partial(halo_kernel, lax.axis_size("tile")),
+        out_shape=jax.ShapeDtypeStruct(rims.shape, rims.dtype),
+        in_specs=[vmem],
+        out_specs=vmem,
+        scratch_shapes=[
+            pltpu.VMEM(rims.shape, rims.dtype),
+            pltpu.SemaphoreType.DMA((2,)),
+            pltpu.SemaphoreType.DMA((2,)),
+        ],
+        compiler_params=pltpu.CompilerParams(collective_id=0, has_side_effects=True),
+    )(rims)
+
+
+def plan(dp_count, tile_count):
+    low = 1
+    while tile_count * low * 2 <= 8 and dp_count % (low * 2) == 0:
+        low *= 2
+    left, radices = dp_count // low, []
+    while left > 1:
+        radix = 4 if left % 4 == 0 else 2 if left % 2 == 0 else left
+        radices.append(radix)
+        left //= radix
+    return low, radices
+
+
+def total_kernel(
+    tile_count, low, radices, factor, weight_ref, rims_ref, sum_ref, rims_out_ref,
+    landed, first_s, stage_s, gather_s, rim_sems, first_sems, stage_sems, gather_sems,
+):
+    dp, tile = lax.axis_index("dp"), lax.axis_index("tile")
+    size = low * tile_count
+    share = weight_ref.shape[0] // size
+    own = lax.rem(dp, low) * tile_count + tile
+    inner = []
+    for step in range(1, size):
+        place = lax.rem(own + step, size)
+        inner.append((place, (dp - lax.rem(dp, low) + place // tile_count, lax.rem(place, tile_count))))
+    outer, unit = [], low
+    for radix in radices:
+        digit = lax.rem(dp // unit, radix)
+        peers = [
+            (dp + (lax.rem(digit + step, radix) - digit) * unit, tile) for step in range(1, radix)
+        ]
+        outer.append((digit, peers))
+        unit *= radix
+    near = Neighbours(tile_count, rims_ref, landed, rim_sems.at[0], rim_sems.at[1])
+
+    greet([peer for _, peer in inner] + [peer for _, peers in outer for peer in peers])
+    copies = []
+    first = []
+    for step, (place, peer) in enumerate(inner):
+        start = pl.multiple_of(place * share, 8)
+        first.append(
+            push(weight_ref.at[pl.ds(start, share)], first_s.at[step], first_sems.at[0, step], first_sems.at[1, step], peer)
+        )
+        first[-1].start()
+    near.start()
+    total = weight_ref[pl.ds(pl.multiple_of(own * share, 8), share), :]
+    for step in range(size - 1):
+        first[step].wait_recv()
+        total = total + first_s[step]
+    copies += first
+
+    for stage, (digit, peers) in enumerate(outer):
+        stage_s[stage, digit] = total
+        moves = []
+        for step, peer in enumerate(peers):
+            slot = stage_s.at[stage, digit]
+            moves.append(push(slot, slot, stage_sems.at[0, stage, step], stage_sems.at[1, stage, step], peer))
+            moves[-1].start()
+        for move in moves:
+            move.wait_recv()
+        total = stage_s[stage, 0]
+        for place in range(1, radices[stage]):
+            total = total + stage_s[stage, place]
+        copies += moves
+
+    gather_s[own] = total * factor
+    moves = []
+    for step, (_, peer) in enumerate(inner):
+        slot = gather_s.at[own]
+        moves.append(push(slot, slot, gather_sems.at[0, step], gather_sems.at[1, step], peer))
+        moves[-1].start()
+    near.finish(rims_out_ref)
+    for move in moves:
+        move.wait_recv()
+    for place in range(size):
+        sum_ref[place * share : (place + 1) * share, :] = gather_s[place]
+    for copy in copies + moves:
+        copy.wait_send()
+
+
+def total_weight(weight_part, rims, pixel_count):
+    dp_count, tile_count = lax.axis_size("dp"), lax.axis_size("tile")
+    low, radices = plan(dp_count, tile_count)
+    size = low * tile_count
+    rows, cols = weight_part.shape
+    widest = max(radices + [2])
+    stages = max(len(radices), 1)
+    share = -(-rows // (8 * size)) * 8
+    weight_part = jnp.pad(weight_part, ((0, share * size - rows), (0, 0)))
+    vmem = pl.BlockSpec(memory_space=pltpu.VMEM)
+    others = max(size - 1, 1)
+    dma = pltpu.SemaphoreType.DMA
+    total, rims = pl.pallas_call(
+        functools.partial(total_kernel, tile_count, low, tuple(radices), pixel_count ** (-0.5)),
+        out_shape=[
+            jax.ShapeDtypeStruct(weight_part.shape, F32),
+            jax.ShapeDtypeStruct(rims.shape, F32),
+        ],
+        in_specs=[vmem] * 2,
+        out_specs=[vmem] * 2,
+        scratch_shapes=[
+            pltpu.VMEM(rims.shape, F32),
+            pltpu.VMEM((others, share, cols), F32),
+            pltpu.VMEM((stages, widest, share, cols), F32),
+            pltpu.VMEM((size, share, cols), F32),
+            dma((2, 2)),
+            dma((2, others)),
+            dma((2, stages, widest - 1)),
+            dma((2, others)),
+        ],
+        compiler_params=pltpu.CompilerParams(
+            collective_id=1, has_side_effects=True, vmem_limit_bytes=40 * 1024 * 1024
+        ),
+    )(weight_part, rims)
+    return total[:rows], rims
 
 
 def shards(frames, features, cotangent, head_weight):
@@ -219,20 +434,26 @@
     upstream = cotangent[0]
     lead = image.shape[:2]
 
+    rim_size = -(-(channels + lead[0] * lead[1] * rim) // 16) * 16
+
     def packed(rim_rows, row):
-        return jnp.concatenate([rim_rows.reshape(-1, cols), row.reshape(-1, cols)], 0)
+        both = jnp.concatenate([row.reshape(-1, cols), rim_rows.reshape(-1, cols)], 0)
+        return jnp.pad(both, ((0, rim_size - both.shape[0]), (0, 0)))
 
     def unpacked(value):
-        split = lead[0] * lead[1] * rim
-        return value[:split].reshape(lead + (rim, cols)), value[split:].reshape(channels, 1, cols)
-
-    before, after = both_ways(
-        packed(image[:, :, :rim], feature_map[:, :1]),
-        packed(image[:, :, rows - rim :], feature_map[:, rows - 1 :]),
-        "tile",
-    )
-    image_before, row_before = unpacked(before)
-    image_after, row_after = unpacked(after)
+        used = channels + lead[0] * lead[1] * rim
+        return value[channels:used].reshape(lead + (rim, cols)), value[:channels].reshape(channels, 1, cols)
+
+    halo = exchange_halo(
+        jnp.stack(
+            [
+                packed(image[:, :, :rim], feature_map[:, :1]),
+                packed(image[:, :, rows - rim :], feature_map[:, rows - 1 :]),
+            ]
+        )
+    )
+    image_before, row_before = unpacked(halo[0])
+    image_after, row_after = unpacked(halo[1])
     extra = -(rows + 2 * rim) % 8
     extra += 0 if rows + 2 * rim + extra >= rows + padded_taps - 1 else 8
     frame_wide = jnp.concatenate(
@@ -242,56 +463,27 @@
         channels, (rows + 2) * cols
     )
     by_group = head_weight.reshape(2, 2, taps, -1)
-
-    def in_groups(vertical, horizontal, front):
-        gap = padded_taps - taps
-        return jnp.concatenate(
-            [
-                jnp.pad(vertical[:, None], ((0, 0), (0, 0), (0, gap), (0, 0))),
-                jnp.pad(horizontal[:, None], ((0, 0), (0, 0), (front, gap - front), (0, 0))),
-            ],
-            1,
-        ).reshape(4 * padded_taps, -1)
-
-    back_front = mirror_front(taps, cols)
-    padded_weight = in_groups(by_group[:, 0], by_group[:, 1], forward_front(taps))
-    mirror_weight = in_groups(by_group[:, 0], by_group[:, 1, ::-1], back_front)
-
-    weight_parts, feat_mid, feat_rims, image_grad = local_grads(
-        feature_flat, frame_wide, upstream, padded_weight, mirror_weight, taps
-    )
-    before, after = both_ways(
-        packed(image_grad[:, :, :rim], feat_rims[0]),
-        packed(image_grad[:, :, rows + rim : rows + 2 * rim], feat_rims[1]),
-        "tile",
-    )
-    image_before, row_before = unpacked(before)
-    image_after, row_after = unpacked(after)
-    middle = image_grad[:, :, rim : rim + rows]
+    gap = padded_taps - taps
+    front = forward_front(taps)
+    padded_weight = jnp.concatenate(
+        [
+            jnp.pad(by_group[:, :1], ((0, 0), (0, 0), (0, gap), (0, 0))),
+            jnp.pad(by_group[:, 1:], ((0, 0), (0, 0), (front, gap - front), (0, 0))),
+        ],
+        1,
+    ).reshape(4 * padded_taps, -1)
+    flipped_weight = jnp.pad(head_weight, ((0, 4 * gap), (0, 0))).T
+
+    weight_part, feat_mid, rims, middle = local_grads(
+        feature_flat, frame_wide, upstream, padded_weight, flipped_weight, taps, rim_size
+    )
+    pixel_count = lax.axis_size("dp") * lax.axis_size("tile") * rows * cols
+    weight_sum, halo = total_weight(weight_part, rims, pixel_count)
+    image_before, row_before = unpacked(halo[0])
+    image_after, row_after = unpacked(halo[1])
     middle = middle.at[:, :, :rim].add(image_before).at[:, :, rows - rim :].add(image_after)
-    feat_grad = jnp.concatenate(
-        [feat_mid[:, :1] + row_before, feat_mid[:, 1 : rows - 1], feat_mid[:, rows - 1 :] + row_after], 1
-    )
-
-    weight_part = weight_parts
-    for axis in ("dp", "tile"):
-        count = lax.axis_size(axis)
-        step = 1
-        while step < count:
-            weight_part = weight_part + lax.ppermute(
-                weight_part, axis, [(i, i ^ step) for i in range(count)]
-            )
-            step *= 2
-    weight_sum = weight_part.transpose(1, 0, 2).reshape(2, 2, padded_taps, -1)
-    weight_sum = jnp.concatenate(
-        [
-            weight_sum[:, :1, :taps],
-            weight_sum[:, 1:, back_front : back_front + taps][:, :, ::-1],
-        ],
-        1,
-    ).reshape(4 * taps, -1)
-    pixel_count = lax.axis_size("dp") * lax.axis_size("tile") * rows * cols
-    return (weight_sum * pixel_count ** (-0.5), feat_grad[None], middle[None])
+    feat_grad = feat_mid.at[:, :1].add(row_before).at[:, rows - 1 :].add(row_after)
+    return (weight_sum[:, : 4 * taps].T, feat_grad[None], middle[None])
 
 
 def solution(mesh):

time: 73.6 us -> 46.6 us (0.63)
  waiting for transfers between devices: 39 us -> 0 us
  Pallas kernels: 4.47 us -> 35.6 us
  starting transfers between devices: 21.4 us -> 0 us
  local copies, waits for them, and re-layouts: 5.79 us -> 8.83 us
    ppermute x9 -> x0, waiting for transfers between devices: 39 us -> none  [the longest x5 36.1 us: shards(): lax.ppermute(weight_part, axis, [(i, i ^ step) for i in range(count)])]
    pallas_call x0 -> x2, Pallas kernels: none -> 25.8 us  [the longest x1 19.4 us: total_weight(): pl.pallas_call(functools.partial(total_kernel, tile_count, low, tuple(rad...]
    ppermute x9 -> x0, starting transfers between devices: 21.4 us -> none  [the longest x5 9.62 us: shards(): lax.ppermute(weight_part, axis, [(i, i ^ step) for i in range(count)])]
    pallas_call x1, Pallas kernels: 4.47 us -> 9.78 us  [local_grads(): pl.pallas_call(functools.partial(local_kernel, tap_count), out_shape=[jax...]
    unnamed x9 -> x17, local copies, waits for them, and re-layouts: 2.38 us -> 5.71 us
    broadcast_in_dim x2 -> x1, other arithmetic: 0.92 us -> 0.01 us  [shards(): return (weight_sum[:, :4 * taps].T, feat_grad[None], middle[None])]
    mul x1 -> x0, local copies, waits for them, and re-layouts: 0.75 us -> none  [shards(): return (weight_sum * pixel_count ** (-0.5), feat_grad[None], middle[None])]
    slice x12 -> x4, local copies, waits for them, and re-layouts: 0.95 us -> 1.59 us  [the longest x1 0.82 us: shards(): image[:, :, :rim]]
  transfers between devices with their start and end apart: 9 -> 0, of which waited for: 7 -> 0; matrix products, arithmetic and copies ran while one was open for 3% -> 0% of each run, Pallas kernels for 0% -> 0%
where the time goes in v2:
time: 46.6 us; the launch traced here: 46.1 us
  Pallas kernels  35.6 us (76%)
  local copies, waits for them, and re-layouts  8.83 us (19%)
  between operations  0.86 us (2%)
  other arithmetic  0.84 us (2%)
    pallas_call x1, Pallas kernels, total_weight(): pl.pallas_call(functools.partial(total_kernel, tile_count, low, tuple(rad...  19.4 us
    pallas_call x1, Pallas kernels, local_grads(): pl.pallas_call(functools.partial(local_kernel, tap_count), out_shape=[jax...  9.78 us
    pallas_call x1, Pallas kernels, exchange_halo(): pl.pallas_call(functools.partial(halo_kernel, lax.axis_size('tile')), out...  6.41 us
    unnamed x17, local copies, waits for them, and re-layouts  5.71 us

profile of v2, /device:TPU:0, one launch (start us, length us, event | category | flops | bytes accessed | tf_op | source)
XLA Modules:
  0.0 46.1 jit_solution(13516290501507117696)
XLA Ops:
  0.6 0.0 copy-start.1
  0.7 0.1 pad.37.clone
  0.7 0.8 %fusion.18 = (bf16[2,3,13,128]{3,2,1,0:T(8,128)(2,1)S(1)}, bf16[2,3,13,128]{3,2,1,0:T(8,128)(2,1)S(1)}) fusion(bf16[2,3,16,128]{3,2,1,0:T(8,128)(2,1)} %bitcast.44), kind=kLoop, calls=%fused_computation.36 | loop fusion | bytes 79872 | tf_op jit(solution)/shard_map/slice | solution.py:450
  1.6 0.0 copy-done.1
  1.6 0.2 copy.16
  1.8 0.1 reshape.210
  1.9 0.0 copy-start.2
  2.0 0.9 %copy-done.2 = bf16[1,64,16,128]{3,2,1,0:T(8,128)(2,1)S(1)} copy-done((bf16[1,64,16,128]{3,2,1,0:T(8,128)(2,1)S(1)}, bf16[1,64,16,128]{3,2,1,0:T(8,128)(2,1)}, u32[]{:S(2)}) %copy-start.2) | copy-done | bytes 262168
  2.8 0.1 copy.24
  2.9 0.6 %pad_maximum_fusion.rims_ref = bf16[2,144,128]{2,1,0:T(8,128)(2,1)} fusion(bf16[1,144,128]{2,1,0:T(8,128)(2,1)S(1)} %get-tuple-element.82, bf16[1,144,128]{2,1,0:T(8,128)(2,1)S(1)} %get-tuple-element.81), kind=kLoop, calls=%fused_computation.15 | loop fusion | flops 36864 | bytes 147456 | tf_op jit(solution)/shard_map/stack | solution.py:448
  3.6 6.4 %shard_map.67 = bf16[2,144,128]{2,1,0:T(8,128)(2,1)} custom-call(bf16[2,144,128]{2,1,0:T(8,128)(2,1)} %pad_maximum_fusion.rims_ref), custom_call_target="tpu_custom_call" | custom-call | tf_op jit(solution)/shard_map/pallas_call | solution.py:297
  10.0 0.7 %slice_bitcast_fusion.4 = (bf16[64,1,128]{2,0,1:T(8,128)(2,1)S(1)}, bf16[64,1,128]{2,0,1:T(8,128)(2,1)S(1)}) fusion(bf16[2,144,128]{2,1,0:T(8,128)(2,1)} %shard_map.67), kind=kLoop, calls=%fused_computation.32 | loop fusion | bytes 65536 | tf_op jit(solution)/shard_map/reshape | solution.py:445
  10.7 0.7 %fusion.17 = (bf16[1,78,128]{2,1,0:T(8,128)(2,1)S(1)}, bf16[1,78,128]{2,1,0:T(8,128)(2,1)S(1)}) fusion(bf16[2,144,128]{2,1,0:T(8,128)(2,1)} %shard_map.67), kind=kLoop, calls=%fused_computation.35 | loop fusion | bytes 79872 | tf_op jit(solution)/shard_map/slice | solution.py:445
  11.5 0.0 copy-start.3
  11.6 0.7 %copy-done.3 = bf16[1,2,3,16,128]{4,3,2,1,0:T(8,128)(2,1)S(1)} copy-done((bf16[1,2,3,16,128]{4,3,2,1,0:T(8,128)(2,1)S(1)}, bf16[1,2,3,16,128]{4,3,2,1,0:T(8,128)(2,1)}, u32[]{:S(2)}) %copy-start.3) | copy-done | bytes 24600
  12.3 0.0 copy-start
  12.3 0.1 maximum_convert_fusion.frame_ref
  12.4 0.7 %copy-done = f32[1,3,16,128]{3,2,1,0:T(8,128)S(1)} copy-done((f32[1,3,16,128]{3,2,1,0:T(8,128)S(1)}, f32[1,3,16,128]{3,2,1,0:T(8,128)}, u32[]{:S(2)}) %copy-start) | copy-done | bytes 24600
  13.0 9.8 %shard_map.68 = (f32[576,128]{1,0:T(8,128)S(1)}, f32[64,16,128]{2,1,0:T(8,128)S(1)}, f32[2,144,128]{2,1,0:T(8,128)S(1)}, f32[2,3,16,128]{3,2,1,0:T(8,128)}) custom-call(bf16[64,2304]{1,0:T(8,128)(2,1)S(1)} %copy_bitcast_fusion.feat_ref, f32[2,3,48,128]{3,2,1,0:T(8,128)S(1)} %maximum_convert_fusion.frame_ref, f32[3,16,128]{2,1,0:T(8,128)S(1)} %bitcast.40, ...), custom_call_target="tpu_custom_call" | custom-call | tf_op jit(solution)/shard_map/pallas_call | solution.py:207
  22.8 19.4 %shard_map.69 = (f32[576,128]{1,0:T(8,128)S(1)}, f32[2,144,128]{2,1,0:T(8,128)S(1)}) custom-call(f32[576,128]{1,0:T(8,128)S(1)} %get-tuple-element.57.weight_ref, f32[2,144,128]{2,1,0:T(8,128)S(1)} %get-tuple-element.58.rims_ref), custom_call_target="tpu_custom_call" | custom-call | tf_op jit(solution)/shard_map/pallas_call | solution.py:402
  42.2 0.9 %copy.19 = f32[108,576]{1,0:T(8,128)} copy(f32[108,576]{0,1:T(8,128)S(1)} %slice_bitcast_fusion) | data formatting | bytes 497664
  43.1 0.0 copy-start.4
  43.1 0.8 %copy-done.4 = f32[2,3,16,128]{3,2,1,0:T(8,128)S(1)} copy-done((f32[2,3,16,128]{3,2,1,0:T(8,128)S(1)}, f32[2,3,16,128]{3,2,1,0:T(8,128)}, u32[]{:S(2)}) %copy-start.4) | copy-done | bytes 49176
  43.9 0.2 scatter-add.16
  44.1 0.2 scatter-add.19
  44.3 0.0 copy-start.5
  44.3 0.2 copy.18
  44.5 0.4 copy-done.5
  45.0 1.1 %copy.20 = f32[1,64,16,128]{3,2,1,0:T(8,128)} copy(f32[1,64,16,128]{3,1,2,0:T(8,128)S(1)} %fusion.13) | data formatting | bytes 1048576
  (20 shorter events, 0.3 us)
Async XLA Ops:
  0.6 1.0 %copy-start.1 = (bf16[108,576]{1,0:T(8,128)(2,1)S(1)}, bf16[108,576]{1,0:T(8,128)(2,1)}, u32[]{:S(2)}) copy-start(bf16[108,576]{1,0:T(8,128)(2,1)} %param.15) | copy-start | bytes 373252
  1.9 1.0 %copy-start.2 = (bf16[1,64,16,128]{3,2,1,0:T(8,128)(2,1)S(1)}, bf16[1,64,16,128]{3,2,1,0:T(8,128)(2,1)}, u32[]{:S(2)}) copy-start(bf16[1,64,16,128]{3,2,1,0:T(8,128)(2,1)} %param.13) | copy-start | bytes 786436
  11.5 0.7 %copy-start.3 = (bf16[1,2,3,16,128]{4,3,2,1,0:T(8,128)(2,1)S(1)}, bf16[1,2,3,16,128]{4,3,2,1,0:T(8,128)(2,1)}, u32[]{:S(2)}) copy-start(bf16[1,2,3,16,128]{4,3,2,1,0:T(8,128)(2,1)} %param.12) | copy-start | bytes 73732
  12.3 0.7 %copy-start = (f32[1,3,16,128]{3,2,1,0:T(8,128)S(1)}, f32[1,3,16,128]{3,2,1,0:T(8,128)}, u32[]{:S(2)}) copy-start(f32[1,3,16,128]{3,2,1,0:T(8,128)} %param.14) | copy-start | bytes 73732
  43.1 0.8 %copy-start.4 = (f32[2,3,16,128]{3,2,1,0:T(8,128)S(1)}, f32[2,3,16,128]{3,2,1,0:T(8,128)}, u32[]{:S(2)}) copy-start(f32[2,3,16,128]{3,2,1,0:T(8,128)} %get-tuple-element.62) | copy-start | bytes 147460
  44.3 0.6 %copy-start.5 = (f32[1,2,3,16,128]{4,3,2,1,0:T(8,128)}, f32[1,2,3,16,128]{4,3,2,1,0:T(8,128)S(1)}, u32[]{:S(2)}) copy-start(f32[1,2,3,16,128]{4,3,2,1,0:T(8,128)S(1)} %scatter-add.19) | copy-start | bytes 147460
